TPU v7x, 32 devices: a whole 2x2x4 slice. The times are simulated.
32 devices in a mesh: ctx: 16 (over z, y, x), head: 2 (over core).
Axes of the slice: x: 2, y: 2, z: 4, core: 2. Of those that a mesh axis runs over, the one named last changes fastest.
Arguments:
- queries: bfloat16 [4096, 8192], P(('ctx', 'head')), may hold values from -64 to 64
- keys: bfloat16 [4096, 1024], P(('ctx', 'head')), may hold values from -64 to 64
- values: bfloat16 [4096, 1024], P(('ctx', 'head')), may hold values from -6 to 6
- doc_lengths: int32 [12], replicated, may hold values from 1 to 1024, as said below
Outputs:
- attended: bfloat16 [4096, 8192], P(('ctx', 'head'))
Inputs may be any that keep to these rules, and one draw needn't show every extreme that they name: `doc_lengths`: the lengths sum to 4096; the first document has one token, the second exactly 1024, and no other more than 1024.
All inputs are finite; a program needn't handle non-finite values.
Results may differ from a plain program's by a relative error of at most 0.004.
Values may be sent and summed in bfloat16 or wider, within the bound.
No kernel may reach another device: no remote copies, remote signals or barrier semaphores. Data moves between devices by JAX's collectives and lax.ppermute only.
A program may use at most 64 MiB of HBM per device.

v0:
```python
import functools
import math

import jax
import jax.numpy as jnp
from jax import lax
from jax.experimental import pallas as pl
from jax.experimental.pallas import tpu as pltpu
from jax.sharding import PartitionSpec as P

HD = 128
REACH = 4
NEVER = -1e30
SCORE_SCALE = HD ** (-0.5) * math.log2(math.e)
SUM_ROWS = 16
PARTS = 2
AXES = ("ctx", "head")
SHIFT, SHIFT_OPPOSITE, OPPOSITE = "shift", "shift opposite", REACH - 1
ROUNDS = ((SHIFT, OPPOSITE), (OPPOSITE, SHIFT), (1, 2), (2, SHIFT_OPPOSITE), (SHIFT_OPPOSITE, 1))


def send_round(block, kinds):
    spans, cores = lax.axis_size("ctx"), lax.axis_size("head")
    pairs = []
    for s in range(spans):
        for core, kind in enumerate(kinds):
            if kind in (SHIFT, SHIFT_OPPOSITE):
                target = s + REACH
                if target >= spans or (kind == SHIFT_OPPOSITE and s % REACH >= REACH // 2):
                    continue
            else:
                target = s ^ kind
            pairs.append((s * cores + core, target * cores + core))
    return lax.ppermute(block, AXES, pairs)


def to_other_core(block):
    cores = lax.axis_size("head")
    return lax.ppermute(block, "head", [(h, cores - 1 - h) for h in range(cores)])


def doc_starts(lengths_ref, first, last):
    def one_doc(i, carry):
        start, lo_first, lo_last = carry
        start = start + lengths_ref[i]
        return start, jnp.where(start <= first, start, lo_first), jnp.where(start <= last, start, lo_last)

    zero = jnp.int32(0)
    _, lo_first, lo_last = lax.fori_loop(0, lengths_ref.shape[0], one_doc, (zero, zero, zero))
    return lo_first, lo_last


def doc_start_rows(lengths_ref, first_query, keys, rows):
    pos = first_query + lax.broadcasted_iota(jnp.int32, (8, rows), 1)

    def one_doc(i, carry):
        start, lo = carry
        start = start + lengths_ref[i]
        return start, jnp.where(start <= pos, start, lo)

    zero = jnp.zeros((8, rows), jnp.int32)
    lo = lax.fori_loop(0, lengths_ref.shape[0], one_doc, (jnp.int32(0), zero))[1]
    return jnp.concatenate([lo] * (keys // 8), axis=0)


def lanes(at, width):
    return pl.ds(pl.multiple_of(at * width, width), width)


def positions(starts, rows):
    return jnp.concatenate([start + lax.broadcasted_iota(jnp.int32, (rows, rows), 0) for start in starts], axis=0)


def turned(block, count):
    width = block.shape[1] // count
    return jnp.concatenate([block[:, i * width : (i + 1) * width].T for i in range(count)], axis=1)


def softmax_step(scores, allowed, max_before):
    if allowed is not None:
        allowed = jnp.concatenate([allowed] * (scores.shape[1] // allowed.shape[1]), axis=1)
        scores = jnp.where(allowed, scores, NEVER)
    row_max = jnp.max(scores, axis=0, keepdims=True)
    rescale = None
    if max_before is not None:
        row_max = jnp.maximum(max_before, row_max)
        rescale = jnp.exp2((max_before - row_max) * SCORE_SCALE)
    return jnp.exp2((scores - row_max) * SCORE_SCALE).astype(jnp.bfloat16), row_max, rescale


def pipeline(kv_heads, ahead_ref, allowed, scores_of, values_of, before_of, store):
    def finish(g, part, scores):
        max_before, acc_before = before_of(g, part)
        weights, row_max, rescale = softmax_step(scores, allowed, max_before)
        values = values_of(g)
        widened = jnp.concatenate([values.T, jnp.ones((SUM_ROWS, values.shape[0]), values.dtype)], axis=0)
        acc = jnp.dot(widened, weights, preferred_element_type=jnp.float32)
        if rescale is not None:
            acc = acc_before * rescale + acc
        store(g, part, row_max, acc)

    ahead_ref[...] = scores_of(0, 0)

    def one_head(g, _):
        scores = ahead_ref[...]
        for part in range(PARTS):
            if part + 1 < PARTS:
                later = scores_of(g, part + 1)
            else:
                later = scores_of(jnp.minimum(g + 1, kv_heads - 1), 0)
            finish(g, part, scores)
            scores = later
        ahead_ref[...] = scores
        return 0

    lax.fori_loop(0, kv_heads, one_head, 0)


def pick_kernel(place_ref, q_ref, out_ref, sem):
    copy = pltpu.make_async_copy(q_ref.at[:, lanes(1 - place_ref[2], out_ref.shape[1])], out_ref, sem)
    copy.start()
    copy.wait()


def own_kernel(place_ref, lengths_ref, q_ref, kv_ref, *refs, side):
    if side == 0:
        qt_ref, max_ref, acc_ref, ahead_ref, q_side_ref, sem = refs
        fetch = pltpu.make_async_copy(q_ref.at[:, lanes(place_ref[2], q_side_ref.shape[1])], q_side_ref, sem)
        fetch.start()
    else:
        _, _, _, qt_ref, max_ref, acc_ref, ahead_ref = refs
        q_side_ref = q_ref
    rows, wide = q_side_ref.shape
    kv_heads = kv_ref.shape[3] // HD
    group_size = wide // (kv_heads * HD)
    width = group_size * rows // PARTS
    half = place_ref[2]
    first, other = place_ref[side], place_ref[1 - side]
    query_pos = first + lax.broadcasted_iota(jnp.int32, (rows, rows), 1)
    lows = doc_start_rows(lengths_ref, first, rows, rows)
    key_pos = positions([first], rows)
    diagonal = (key_pos >= lows) & (key_pos <= query_pos)
    earlier = positions([other], rows) >= lows
    if side == 0:
        fetch.wait()

    def at(g, part):
        return lanes((side * kv_heads + g) * PARTS + part, width)

    def turn_queries(g, _):
        for part in range(PARTS):
            q = q_side_ref[:, lanes(g * PARTS + part, group_size // PARTS * HD)]
            qt_ref[:, at(g, part)] = turned(q, group_size // PARTS)
        return 0

    lax.fori_loop(0, kv_heads, turn_queries, 0)

    def store(g, part, row_max, acc):
        max_ref[:, at(g, part)] = jnp.broadcast_to(row_max, (8, width))
        acc_ref[:, at(g, part)] = acc

    def work(blocks, allowed):
        def of(i, g):
            return jnp.concatenate([kv_ref[block, i, :, lanes(g, HD)] for block in blocks], axis=0)

        pipeline(
            kv_heads,
            ahead_ref.at[: len(blocks) * rows],
            allowed,
            lambda g, part: jnp.dot(of(0, g), qt_ref[:, at(g, part)], preferred_element_type=jnp.float32),
            lambda g: of(1, g),
            lambda g, part: (None, None),
            store,
        )

    pl.when(half == side)(lambda: work([side], diagonal))
    pl.when(half != side)(lambda: work([1 - side, side], jnp.concatenate([earlier, diagonal], axis=0)))


def span_steps(place_ref, lengths_ref, kv_ref, qt_ref, ahead_ref, number, side, load, store):
    rows = kv_ref.shape[2]
    kv_heads = kv_ref.shape[3] // HD
    width = qt_ref.shape[1] // (2 * kv_heads * PARTS)
    first = place_ref[side]
    key_starts = place_ref[3 + 2 * number], place_ref[4 + 2 * number]
    lo_first, lo_last = doc_starts(lengths_ref, first, first + rows - 1)
    needed = jnp.maximum(key_starts[0], key_starts[1]) + rows > lo_first
    whole = jnp.minimum(key_starts[0], key_starts[1]) >= lo_last

    def at(g, part):
        return lanes((side * kv_heads + g) * PARTS + part, width)

    def of(i, g):
        return jnp.concatenate([kv_ref[block, i, :, lanes(g, HD)] for block in range(2)], axis=0)

    def work(masked):
        allowed = None
        if masked:
            allowed = positions(key_starts, rows) >= doc_start_rows(lengths_ref, first, 2 * rows, rows)
        pipeline(
            kv_heads,
            ahead_ref,
            allowed,
            lambda g, part: jnp.dot(of(0, g), qt_ref[:, at(g, part)], preferred_element_type=jnp.float32),
            lambda g: of(1, g),
            lambda g, part: load(at(g, part)),
            lambda g, part, row_max, acc: store(g, part, at(g, part), row_max, acc),
        )

    pl.when(whole)(lambda: work(False))
    pl.when(needed & jnp.logical_not(whole))(lambda: work(True))
    return needed


def span_kernel(place_ref, lengths_ref, *refs, numbers):
    kv_refs, (qt_ref, _, _, max_ref, acc_ref, ahead_ref) = refs[: len(numbers)], refs[len(numbers) :]

    def load(at):
        return max_ref[:1, at], acc_ref[:, at]

    def store(g, part, at, row_max, acc):
        max_ref[:, at] = jnp.broadcast_to(row_max, (8, acc.shape[1]))
        acc_ref[:, at] = acc

    for number, kv_ref in zip(numbers, kv_refs):

        def one_side(side, _):
            span_steps(place_ref, lengths_ref, kv_ref, qt_ref, ahead_ref, number, side, load, store)
            return 0

        lax.fori_loop(0, 2, one_side, 0)


def last_kernel(place_ref, lengths_ref, kv_ref, qt_ref, max_ref, acc_ref, out_ref, ahead_ref, *refs, number, side):
    rows = kv_ref.shape[2]
    kv_heads = kv_ref.shape[3] // HD
    width = qt_ref.shape[1] // (2 * kv_heads * PARTS)
    out = out_ref
    if refs:
        out, sem = refs

    def load(at):
        return max_ref[:1, at], acc_ref[:, at]

    def finish(g, part, at, row_max, acc):
        finished = (acc[:HD] * (1.0 / acc[HD : HD + 1])).astype(out.dtype)
        out[:, lanes(g * PARTS + part, width)] = turned(finished, width // rows)

    needed = span_steps(place_ref, lengths_ref, kv_ref, qt_ref, ahead_ref, number, side, load, finish)

    @pl.when(jnp.logical_not(needed))
    def _():
        def one_head(g, _):
            for part in range(PARTS):
                finish(g, part, None, *load(lanes((side * kv_heads + g) * PARTS + part, width)))
            return 0

        lax.fori_loop(0, kv_heads, one_head, 0)

    if refs:
        copy = pltpu.make_async_copy(out, out_ref.at[:, lanes(place_ref[2], out.shape[1])], sem)
        copy.start()
        copy.wait()


def join_kernel(place_ref, far_ref, out_in, out_ref, sem):
    del out_in
    copy = pltpu.make_async_copy(far_ref, out_ref.at[:, lanes(1 - place_ref[2], far_ref.shape[1])], sem)
    copy.start()
    copy.wait()


def per_device(queries, keys, values, doc_lengths):
    rows, all_heads = queries.shape
    half_heads = all_heads // 2
    head_rows = (all_heads // HD) * rows
    half, span = lax.axis_index("head"), lax.axis_index("ctx")
    cores = lax.axis_size("head")
    place_in_group = lax.rem(span, REACH)

    nowhere = -2 * REACH

    def origin(kind):
        if kind == SHIFT:
            return span - REACH
        late = place_in_group >= REACH // 2
        from_place = place_in_group ^ (OPPOSITE if kind == SHIFT_OPPOSITE else kind)
        here = span - place_in_group + from_place
        if kind == SHIFT_OPPOSITE:
            return jnp.where(late, nowhere, here - REACH)
        if kind == OPPOSITE:
            return jnp.where(late, here, nowhere)
        return here - jnp.where(from_place > place_in_group, REACH, 0)

    parts = [(span * cores + half) * rows, (span * cores + 1 - half) * rows, half]
    for kinds in ROUNDS:
        start = jnp.where(half == 0, origin(kinds[0]), origin(kinds[1]))
        parts += [(start * cores + half) * rows, (start * cores + 1 - half) * rows]
    place = jnp.stack(parts).astype(jnp.int32)

    vmem = pl.BlockSpec(memory_space=pltpu.VMEM)
    smem = pl.BlockSpec(memory_space=pltpu.SMEM)
    anywhere = pl.BlockSpec(memory_space=pl.ANY)
    hbm = pl.BlockSpec(memory_space=pltpu.MemorySpace.HBM)
    qt_shape = jax.ShapeDtypeStruct((HD, head_rows), queries.dtype)
    max_shape = jax.ShapeDtypeStruct((8, head_rows), jnp.float32)
    acc_shape = jax.ShapeDtypeStruct((HD + SUM_ROWS, head_rows), jnp.float32)
    side_shape = jax.ShapeDtypeStruct((rows, half_heads), queries.dtype)
    common = dict(
        compiler_params=pltpu.CompilerParams(vmem_limit_bytes=24 * 1024 * 1024),
        cost_estimate=pl.CostEstimate(flops=0, bytes_accessed=0, transcendentals=0),
    )

    def heads_of(array, core):
        width = array.shape[1] // 2
        return lax.dynamic_slice_in_dim(array, core * width, width, 1)

    to_give = jnp.stack([heads_of(keys, 1 - half), heads_of(values, 1 - half)])
    given = to_other_core(to_give)
    given, queries = lax.optimization_barrier((given, queries))
    own = jnp.stack([jnp.stack([heads_of(keys, half), heads_of(values, half)]), given])
    arrived = [send_round(own, kinds) for kinds in ROUNDS[:2]]
    q_far = to_other_core(
        pl.pallas_call(
            pick_kernel,
            in_specs=[smem, hbm],
            out_specs=vmem,
            out_shape=side_shape,
            scratch_shapes=[pltpu.SemaphoreType.DMA],
            name="pick_queries",
            **common,
        )(place, queries)
    )

    group_columns = half_heads // (keys.shape[1] // 2) * rows // PARTS
    ahead = pltpu.VMEM((2 * rows, group_columns), jnp.float32)
    state_shapes = (qt_shape, max_shape, acc_shape)
    state = pl.pallas_call(
        functools.partial(own_kernel, side=0),
        in_specs=[smem, smem, hbm, vmem],
        out_specs=(vmem, vmem, vmem),
        out_shape=state_shapes,
        scratch_shapes=[ahead, pltpu.VMEM((rows, half_heads), queries.dtype), pltpu.SemaphoreType.DMA],
        name="attend_own_near",
        **{**common, "cost_estimate": pl.CostEstimate(flops=10**11, bytes_accessed=0, transcendentals=0)},
    )(place, doc_lengths, queries, own)
    qt, row_max, acc = pl.pallas_call(
        functools.partial(own_kernel, side=1),
        in_specs=[smem, smem] + [vmem] * 5,
        out_specs=(vmem, vmem, vmem),
        out_shape=state_shapes,
        input_output_aliases={4: 0, 5: 1, 6: 2},
        scratch_shapes=[ahead],
        name="attend_own_far",
        **common,
    )(place, doc_lengths, q_far, own, *state)

    def attend(kv, row_max, acc, number):
        return pl.pallas_call(
            functools.partial(span_kernel, numbers=tuple(range(number, number + len(kv)))),
            in_specs=[smem, smem] + [vmem] * (len(kv) + 3),
            out_specs=(vmem, vmem),
            out_shape=(max_shape, acc_shape),
            input_output_aliases={len(kv) + 3: 0, len(kv) + 4: 1},
            scratch_shapes=[ahead],
            name="attend_spans",
            **common,
        )(place, doc_lengths, *kv, qt, row_max, acc)

    arrived[0], arrived[1], acc = lax.optimization_barrier((arrived[0], arrived[1], acc))
    behind = jnp.where(half == 0, arrived[0], arrived[1])
    opposite = jnp.where(half == 0, arrived[1], arrived[0])

    def to_send(kind):
        if kind == SHIFT_OPPOSITE:
            return opposite
        return jnp.where((place_in_group ^ kind) > place_in_group, own, behind)

    for kinds in ROUNDS[2:]:
        arrived.append(send_round(jnp.where(half == 0, to_send(kinds[0]), to_send(kinds[1])), kinds))
    row_max, acc = attend(arrived[:2], row_max, acc, 0)
    row_max, acc = attend(arrived[2:3], row_max, acc, 2)
    row_max, acc = attend(arrived[3:4], row_max, acc, 3)

    last_args = (place, doc_lengths, arrived[4], qt, row_max, acc)
    out_far = pl.pallas_call(
        functools.partial(last_kernel, number=4, side=1),
        in_specs=[smem, smem] + [vmem] * 4,
        out_specs=vmem,
        out_shape=side_shape,
        scratch_shapes=[ahead],
        name="attend_last_far",
        **common,
    )(*last_args)
    out = pl.pallas_call(
        functools.partial(last_kernel, number=4, side=0),
        in_specs=[smem, smem] + [vmem] * 4,
        out_specs=anywhere,
        out_shape=jax.ShapeDtypeStruct(queries.shape, queries.dtype),
        scratch_shapes=[ahead, pltpu.VMEM((rows, half_heads), queries.dtype), pltpu.SemaphoreType.DMA],
        name="attend_last_near",
        **common,
    )(*last_args)
    return pl.pallas_call(
        join_kernel,
        in_specs=[smem, vmem, anywhere],
        out_specs=anywhere,
        out_shape=jax.ShapeDtypeStruct(queries.shape, queries.dtype),
        input_output_aliases={2: 0},
        scratch_shapes=[pltpu.SemaphoreType.DMA],
        name="join_heads",
        **common,
    )(place, to_other_core(out_far), out)


def solution(mesh):
    placed = P(AXES, None)
    return jax.shard_map(
        per_device, mesh=mesh, in_specs=(placed, placed, placed, P()), out_specs=placed, check_vma=False
    )
```

profile of v0, /device:TPU:7, one launch (start us, length us, event | category | flops | bytes accessed | tf_op | source)
XLA Modules:
  0.0 53.1 jit_solution(12960115346804125662)
XLA Ops:
  0.0 0.0 copy-start
  0.0 0.0 copy-start.1
  0.0 1.3 %dynamic-slice_bitcast_fusion.2 = (bf16[1,128,512]{2,1,0:T(8,128)(2,1)S(1)}, bf16[1,128,512]{2,1,0:T(8,128)(2,1)S(1)}, bf16[1,128,512]{2,1,0:T(8,128)(2,1)S(1)}, bf16[1,128,512]{2,1,0:T(8,128)(2,1)S(1)}) fusion(bf16[128,1024]{1,0:T(8,128)(2,1)} %param.6, s32[]{:T(128)S(6)} %select_n.93, s32[]{:T(128)S(6)} %select_n.94, bf16[128,1024]{1,0:T(8,128)(2,1)} %param.5), kind=kLoop, calls=%fused_computation.12 | loop fusion | bytes 1048584 | tf_op jit(solution)/shard_map/stack | solution.py:321
  1.3 0.7 %collective-permute-start = (bf16[2,128,512]{2,1,0:T(8,128)(2,1)S(1)}, bf16[2,128,512]{2,1,0:T(8,128)(2,1)S(1)}, u32[]{:S(2)}, u32[]{:S(2)}) collective-permute-start(bf16[2,128,512]{2,1,0:T(8,128)(2,1)S(1)} %pad_maximum_fusion.1), channel_id=1, source_target_pairs={{0,1},{1,0},{2,3},{3,2},{4,5},{5,4},{6,7},{7,6},{8,9},{9,8},{10,11... | collective-permute-start | bytes 786440 | tf_op jit(solution)/shard_map/ppermute | solution.py:39
  2.1 0.1 stack.82.place_ref
  2.2 1.0 %collective-permute-done = bf16[2,128,512]{2,1,0:T(8,128)(2,1)S(1)} collective-permute-done((bf16[2,128,512]{2,1,0:T(8,128)(2,1)S(1)}, bf16[2,128,512]{2,1,0:T(8,128)(2,1)S(1)}, u32[]{:S(2)}, u32[]{:S(2)}) %collective-permute-start) | collective-permute-done | bytes 262176 | tf_op jit(solution)/shard_map/ppermute | solution.py:39
  3.2 0.1 pad_maximum_fusion.kv_ref
  3.3 1.9 %collective-permute-start.1 = (bf16[2,2,128,512]{3,2,1,0:T(8,128)(2,1)S(1)}, bf16[2,2,128,512]{3,2,1,0:T(8,128)(2,1)S(1)}, u32[]{:S(2)}, u32[]{:S(2)}) collective-permute-start(bf16[2,2,128,512]{3,2,1,0:T(8,128)(2,1)S(1)} %pad_maximum_fusion.kv_ref), channel_id=1, source_target_pairs={{0,8},{1,7},{2,10},{3,5},{4,12},{5,3},{6,14},{7,1},{8,16},{9,15},{... | collective-permute-start | bytes 1572872 | tf_op jit(solution)/shard_map/ppermute | solution.py:34
  5.2 3.4 %collective-permute-start.2 = (bf16[2,2,128,512]{3,2,1,0:T(8,128)(2,1)S(1)}, bf16[2,2,128,512]{3,2,1,0:T(8,128)(2,1)S(1)}, u32[]{:S(2)}, u32[]{:S(2)}) collective-permute-start(bf16[2,2,128,512]{3,2,1,0:T(8,128)(2,1)S(1)} %pad_maximum_fusion.kv_ref), channel_id=1, source_target_pairs={{0,6},{1,9},{2,4},{3,11},{4,2},{5,13},{6,0},{7,15},{8,14},{9,17},{... | collective-permute-start | bytes 1572872 | tf_op jit(solution)/shard_map/ppermute | solution.py:34
  8.6 0.0 copy-done
  8.6 0.6 %pick_queries.1 = bf16[128,4096]{1,0:T(8,128)(2,1)S(1)} custom-call(s32[13]{0:T(128)S(1)} %stack.82.place_ref, bf16[128,8192]{1,0:T(8,128)(2,1)S(1)} %copy-done), custom_call_target="tpu_custom_call" | custom-call | tf_op jit(solution)/shard_map/pick_queries/pallas_call | solution.py:324
  9.3 1.0 %collective-permute-start.3 = (bf16[128,4096]{1,0:T(8,128)(2,1)S(1)}, bf16[128,4096]{1,0:T(8,128)(2,1)S(1)}, u32[]{:S(2)}, u32[]{:S(2)}) collective-permute-start(bf16[128,4096]{1,0:T(8,128)(2,1)S(1)} %pick_queries.1), channel_id=1, source_target_pairs={{0,1},{1,0},{2,3},{3,2},{4,5},{5,4},{6,7},{7,6},{8,9},{9,8},{10,11... | collective-permute-start | bytes 3145736 | tf_op jit(solution)/shard_map/ppermute | solution.py:39
  10.3 0.0 copy-done.1
  10.3 3.7 %attend_own_near.1 = (bf16[128,8192]{1,0:T(8,128)(2,1)S(1)}, f32[8,8192]{1,0:T(8,128)S(1)}, f32[144,8192]{1,0:T(8,128)S(1)}) custom-call(s32[13]{0:T(128)S(1)} %stack.82.place_ref, s32[12]{0:T(128)S(1)} %copy-done.1, bf16[128,8192]{1,0:T(8,128)(2,1)S(1)} %copy-done, bf16[2,2,128,512]{3,2,1,0:T(8,128)(2,1)S(1)} %pad_maximum_fusion.kv_ref), custom_call_target="tpu_custom_call" | custom-call | flops 99999997952 | tf_op jit(solution)/shard_map/attend_own_near/pallas_call | solution.py:338
  14.0 0.0 collective-permute-done.3.q_ref
  14.0 3.0 %attend_own_far.1 = (bf16[128,8192]{1,0:T(8,128)(2,1)S(1)}, f32[8,8192]{1,0:T(8,128)S(1)}, f32[144,8192]{1,0:T(8,128)S(1)}) custom-call(s32[13]{0:T(128)S(1)} %stack.82.place_ref, s32[12]{0:T(128)S(1)} %copy-done.1, bf16[128,4096]{1,0:T(8,128)(2,1)S(1)} %collective-permute-done.3.q_ref, ...), custom_call_target="tpu_custom_call", output_to_operand_aliasing={{0}: (4, {}), {1}: (5, {}), {2}: (6, {})} | custom-call | tf_op jit(solution)/shard_map/attend_own_far/pallas_call | solution.py:347
  17.0 0.0 collective-permute-done.1.refs_0_
  17.0 2.0 %collective-permute-done.2.refs_1_ = bf16[2,2,128,512]{3,2,1,0:T(8,128)(2,1)S(1)} collective-permute-done((bf16[2,2,128,512]{3,2,1,0:T(8,128)(2,1)S(1)}, bf16[2,2,128,512]{3,2,1,0:T(8,128)(2,1)S(1)}, u32[]{:S(2)}, u32[]{:S(2)}) %collective-permute-start.2) | collective-permute-done | bytes 524320 | tf_op jit(solution)/shard_map/ppermute | solution.py:34
  19.0 0.2 broadcast_select_fusion.2
  19.2 0.3 collective-permute-start.6
  19.5 0.7 %collective-permute-start.5 = (bf16[2,2,128,512]{3,2,1,0:T(8,128)(2,1)S(1)}, bf16[2,2,128,512]{3,2,1,0:T(8,128)(2,1)S(1)}, u32[]{:S(2)}, u32[]{:S(2)}) collective-permute-start(bf16[2,2,128,512]{3,2,1,0:T(8,128)(2,1)S(1)} %get-tuple-element.40), channel_id=1, source_target_pairs={{0,4},{1,9},{2,6},{3,11},{4,0},{6,2},{8,12},{9,17},{10,14},{11,19}... | collective-permute-start | bytes 1572872 | tf_op jit(solution)/shard_map/ppermute | solution.py:34
  20.2 2.2 %collective-permute-start.4 = (bf16[2,2,128,512]{3,2,1,0:T(8,128)(2,1)S(1)}, bf16[2,2,128,512]{3,2,1,0:T(8,128)(2,1)S(1)}, u32[]{:S(2)}, u32[]{:S(2)}) collective-permute-start(bf16[2,2,128,512]{3,2,1,0:T(8,128)(2,1)S(1)} %get-tuple-element.41), channel_id=1, source_target_pairs={{0,8},{1,3},{2,10},{3,1},{5,7},{7,5},{8,16},{9,11},{10,18},{11,9},... | collective-permute-start | bytes 1572872 | tf_op jit(solution)/shard_map/ppermute | solution.py:34
  22.4 6.0 %attend_spans.3 = (f32[8,8192]{1,0:T(8,128)S(1)}, f32[144,8192]{1,0:T(8,128)S(1)}) custom-call(s32[13]{0:T(128)S(1)} %stack.82.place_ref, s32[12]{0:T(128)S(1)} %copy-done.1, bf16[2,2,128,512]{3,2,1,0:T(8,128)(2,1)S(1)} %collective-permute-done.1.refs_0_, ...), custom_call_target="tpu_custom_call", output_to_operand_aliasing={{0}: (5, {}), {1}: (6, {})} | custom-call | tf_op jit(solution)/shard_map/attend_spans/pallas_call | solution.py:359
  28.4 0.5 collective-permute-done.6.refs_0_
  28.9 5.7 %attend_spans.4 = (f32[8,8192]{1,0:T(8,128)S(1)}, f32[144,8192]{1,0:T(8,128)S(1)}) custom-call(s32[13]{0:T(128)S(1)} %stack.82.place_ref, s32[12]{0:T(128)S(1)} %copy-done.1, bf16[2,2,128,512]{3,2,1,0:T(8,128)(2,1)S(1)} %collective-permute-done.6.refs_0_, ...), custom_call_target="tpu_custom_call", output_to_operand_aliasing={{0}: (4, {}), {1}: (5, {})} | custom-call | tf_op jit(solution)/shard_map/attend_spans/pallas_call | solution.py:359
  34.6 0.0 collective-permute-done.5.refs_0_
  34.6 0.8 %attend_spans.5 = (f32[8,8192]{1,0:T(8,128)S(1)}, f32[144,8192]{1,0:T(8,128)S(1)}) custom-call(s32[13]{0:T(128)S(1)} %stack.82.place_ref, s32[12]{0:T(128)S(1)} %copy-done.1, bf16[2,2,128,512]{3,2,1,0:T(8,128)(2,1)S(1)} %collective-permute-done.5.refs_0_, ...), custom_call_target="tpu_custom_call", output_to_operand_aliasing={{0}: (4, {}), {1}: (5, {})} | custom-call | tf_op jit(solution)/shard_map/attend_spans/pallas_call | solution.py:359
  35.4 0.0 collective-permute-done.4.kv_ref
  35.4 3.6 %attend_last_far.1 = bf16[128,4096]{1,0:T(8,128)(2,1)S(1)} custom-call(s32[13]{0:T(128)S(1)} %stack.82.place_ref, s32[12]{0:T(128)S(1)} %copy-done.1, bf16[2,2,128,512]{3,2,1,0:T(8,128)(2,1)S(1)} %collective-permute-done.4.kv_ref, bf16[128,8192]{1,0:T(8,128)(2,1)S(1)} %get-tuple-element.30.refs_2_.refs_1_.qt_ref, f32[8,8192]{1,0:T(8,128)S(1)} %get-tuple-element.37.max_ref, ...), custom_call_target="tpu_custom_call" | custom-call | tf_op jit(solution)/shard_map/attend_last_far/pallas_call | solution.py:386
  39.0 8.1 %collective-permute-start.7 = (bf16[128,4096]{1,0:T(8,128)(2,1)S(1)}, bf16[128,4096]{1,0:T(8,128)(2,1)S(1)}, u32[]{:S(2)}, u32[]{:S(2)}) collective-permute-start(bf16[128,4096]{1,0:T(8,128)(2,1)S(1)} %attend_last_far.1), channel_id=1, source_target_pairs={{0,1},{1,0},{2,3},{3,2},{4,5},{5,4},{6,7},{7,6},{8,9},{9,8},{10,11... | collective-permute-start | bytes 3145736 | tf_op jit(solution)/shard_map/ppermute | solution.py:39
  47.0 4.5 %attend_last_near.1.out_in = bf16[128,8192]{1,0:T(8,128)(2,1)} custom-call(s32[13]{0:T(128)S(1)} %stack.82.place_ref, s32[12]{0:T(128)S(1)} %copy-done.1, bf16[2,2,128,512]{3,2,1,0:T(8,128)(2,1)S(1)} %collective-permute-done.4.kv_ref, bf16[128,8192]{1,0:T(8,128)(2,1)S(1)} %get-tuple-element.30.refs_2_.refs_1_.qt_ref, ...), custom_call_target="tpu_custom_call" | custom-call | tf_op jit(solution)/shard_map/attend_last_near/pallas_call | solution.py:395
  51.6 0.0 collective-permute-done.7.far_ref
  51.6 1.5 %join_heads.1 = bf16[128,8192]{1,0:T(8,128)(2,1)} custom-call(s32[13]{0:T(128)S(1)} %stack.82.place_ref, bf16[128,4096]{1,0:T(8,128)(2,1)S(1)} %collective-permute-done.7.far_ref, bf16[128,8192]{1,0:T(8,128)(2,1)} %attend_last_near.1.out_in), custom_call_target="tpu_custom_call", output_to_operand_aliasing={{}: (2, {})} | custom-call | tf_op jit(solution)/shard_map/join_heads/pallas_call | solution.py:404
  (2 shorter events, 0.1 us)
Async XLA Ops:
  0.0 8.6 %copy-start = (bf16[128,8192]{1,0:T(8,128)(2,1)S(1)}, bf16[128,8192]{1,0:T(8,128)(2,1)}, u32[]{:S(2)}) copy-start(bf16[128,8192]{1,0:T(8,128)(2,1)} %q_ref.1) | copy-start | bytes 6291460
  0.0 10.3 %copy-start.1 = (s32[12]{0:T(128)S(1)}, s32[12]{0:T(128)}, u32[]{:S(2)}) copy-start(s32[12]{0:T(128)} %lengths_ref.13) | copy-start | bytes 148
  1.3 1.9 %collective-permute-start = (bf16[2,128,512]{2,1,0:T(8,128)(2,1)S(1)}, bf16[2,128,512]{2,1,0:T(8,128)(2,1)S(1)}, u32[]{:S(2)}, u32[]{:S(2)}) collective-permute-start(bf16[2,128,512]{2,1,0:T(8,128)(2,1)S(1)} %pad_maximum_fusion.1), channel_id=1, source_target_pairs={{0,1},{1,0},{2,3},{3,2},{4,5},{5,4},{6,7},{7,6},{8,9},{9,8},{10,11... | collective-permute-start | bytes 786440 | tf_op jit(solution)/shard_map/ppermute | solution.py:39
  3.3 13.7 %collective-permute-start.1 = (bf16[2,2,128,512]{3,2,1,0:T(8,128)(2,1)S(1)}, bf16[2,2,128,512]{3,2,1,0:T(8,128)(2,1)S(1)}, u32[]{:S(2)}, u32[]{:S(2)}) collective-permute-start(bf16[2,2,128,512]{3,2,1,0:T(8,128)(2,1)S(1)} %pad_maximum_fusion.kv_ref), channel_id=1, source_target_pairs={{0,8},{1,7},{2,10},{3,5},{4,12},{5,3},{6,14},{7,1},{8,16},{9,15},{... | collective-permute-start | bytes 1572872 | tf_op jit(solution)/shard_map/ppermute | solution.py:34
  5.2 13.8 %collective-permute-start.2 = (bf16[2,2,128,512]{3,2,1,0:T(8,128)(2,1)S(1)}, bf16[2,2,128,512]{3,2,1,0:T(8,128)(2,1)S(1)}, u32[]{:S(2)}, u32[]{:S(2)}) collective-permute-start(bf16[2,2,128,512]{3,2,1,0:T(8,128)(2,1)S(1)} %pad_maximum_fusion.kv_ref), channel_id=1, source_target_pairs={{0,6},{1,9},{2,4},{3,11},{4,2},{5,13},{6,0},{7,15},{8,14},{9,17},{... | collective-permute-start | bytes 1572872 | tf_op jit(solution)/shard_map/ppermute | solution.py:34
  9.3 4.7 %collective-permute-start.3 = (bf16[128,4096]{1,0:T(8,128)(2,1)S(1)}, bf16[128,4096]{1,0:T(8,128)(2,1)S(1)}, u32[]{:S(2)}, u32[]{:S(2)}) collective-permute-start(bf16[128,4096]{1,0:T(8,128)(2,1)S(1)} %pick_queries.1), channel_id=1, source_target_pairs={{0,1},{1,0},{2,3},{3,2},{4,5},{5,4},{6,7},{7,6},{8,9},{9,8},{10,11... | collective-permute-start | bytes 3145736 | tf_op jit(solution)/shard_map/ppermute | solution.py:39
  19.2 9.7 %collective-permute-start.6 = (bf16[2,2,128,512]{3,2,1,0:T(8,128)(2,1)S(1)}, bf16[2,2,128,512]{3,2,1,0:T(8,128)(2,1)S(1)}, u32[]{:S(2)}, u32[]{:S(2)}) collective-permute-start(bf16[2,2,128,512]{3,2,1,0:T(8,128)(2,1)S(1)} %get-tuple-element.39), channel_id=1, source_target_pairs={{0,2},{1,5},{2,0},{3,7},{4,6},{5,1},{6,4},{7,3},{8,10},{9,13},{10,... | collective-permute-start | bytes 1572872 | tf_op jit(solution)/shard_map/ppermute | solution.py:34
  19.5 15.1 %collective-permute-start.5 = (bf16[2,2,128,512]{3,2,1,0:T(8,128)(2,1)S(1)}, bf16[2,2,128,512]{3,2,1,0:T(8,128)(2,1)S(1)}, u32[]{:S(2)}, u32[]{:S(2)}) collective-permute-start(bf16[2,2,128,512]{3,2,1,0:T(8,128)(2,1)S(1)} %get-tuple-element.40), channel_id=1, source_target_pairs={{0,4},{1,9},{2,6},{3,11},{4,0},{6,2},{8,12},{9,17},{10,14},{11,19}... | collective-permute-start | bytes 1572872 | tf_op jit(solution)/shard_map/ppermute | solution.py:34
  20.2 15.2 %collective-permute-start.4 = (bf16[2,2,128,512]{3,2,1,0:T(8,128)(2,1)S(1)}, bf16[2,2,128,512]{3,2,1,0:T(8,128)(2,1)S(1)}, u32[]{:S(2)}, u32[]{:S(2)}) collective-permute-start(bf16[2,2,128,512]{3,2,1,0:T(8,128)(2,1)S(1)} %get-tuple-element.41), channel_id=1, source_target_pairs={{0,8},{1,3},{2,10},{3,1},{5,7},{7,5},{8,16},{9,11},{10,18},{11,9},... | collective-permute-start | bytes 1572872 | tf_op jit(solution)/shard_map/ppermute | solution.py:34
  39.0 12.6 %collective-permute-start.7 = (bf16[128,4096]{1,0:T(8,128)(2,1)S(1)}, bf16[128,4096]{1,0:T(8,128)(2,1)S(1)}, u32[]{:S(2)}, u32[]{:S(2)}) collective-permute-start(bf16[128,4096]{1,0:T(8,128)(2,1)S(1)} %attend_last_far.1), channel_id=1, source_target_pairs={{0,1},{1,0},{2,3},{3,2},{4,5},{5,4},{6,7},{7,6},{8,9},{9,8},{10,11... | collective-permute-start | bytes 3145736 | tf_op jit(solution)/shard_map/ppermute | solution.py:39
where the time goes:
time: 53.4 us; the launch traced here: 53.1 us
  Pallas kernels  29.4 us (55%)
  starting transfers between devices  18.3 us (34%)
  waiting for transfers between devices  3.58 us (7%)
  local copies, waits for them, and re-layouts  1.37 us (3%)
    pallas_call x3, Pallas kernels, attend(): pl.pallas_call(functools.partial(span_kernel, numbers=tuple(range(number,...  12.4 us
    ppermute x3, starting transfers between devices, to_other_core(): lax.ppermute(block, 'head', [(h, cores - 1 - h) for h in range(cores)])  9.83 us
    ppermute x5, starting transfers between devices, send_round(): return lax.ppermute(block, AXES, pairs)  8.48 us
    pallas_call x1, Pallas kernels, per_device(): pl.pallas_call(functools.partial(last_kernel, number=4, side=0), in_specs...  4.52 us
    pallas_call x1, Pallas kernels, per_device(): pl.pallas_call(functools.partial(own_kernel, side=0), in_specs=[smem, sme...  3.67 us
    pallas_call x1, Pallas kernels, per_device(): pl.pallas_call(functools.partial(last_kernel, number=4, side=1), in_specs...  3.57 us
    pallas_call x1, Pallas kernels, per_device(): pl.pallas_call(functools.partial(own_kernel, side=1), in_specs=[smem, sme...  3.03 us
    ppermute x5, waiting for transfers between devices, send_round(): return lax.ppermute(block, AXES, pairs)  2.54 us
  transfers between devices with their start and end apart: 8, of which 3 were waited for; matrix products, arithmetic and copies ran while one was open for 0% of the time, Pallas kernels for 46%

commit v1 on v0

--- a/solution.py
+++ b/solution.py
@@ -16,7 +16,7 @@
 PARTS = 2
 AXES = ("ctx", "head")
 SHIFT, SHIFT_OPPOSITE, OPPOSITE = "shift", "shift opposite", REACH - 1
-ROUNDS = ((SHIFT, OPPOSITE), (OPPOSITE, SHIFT), (1, 2), (2, SHIFT_OPPOSITE), (SHIFT_OPPOSITE, 1))
+ROUNDS = ((SHIFT, SHIFT), (OPPOSITE, OPPOSITE), (1, 2), (SHIFT_OPPOSITE, SHIFT_OPPOSITE), (2, 1))
 
 
 def send_round(block, kinds):
@@ -100,20 +100,22 @@
         store(g, part, row_max, acc)
 
     ahead_ref[...] = scores_of(0, 0)
-
-    def one_head(g, _):
+    step = 2 if kv_heads % 2 == 0 else 1
+
+    def some_heads(i, _):
         scores = ahead_ref[...]
-        for part in range(PARTS):
-            if part + 1 < PARTS:
-                later = scores_of(g, part + 1)
+        for number in range(step * PARTS):
+            g, part = i * step + number // PARTS, number % PARTS
+            if number + 1 < step * PARTS:
+                later = scores_of(i * step + (number + 1) // PARTS, (number + 1) % PARTS)
             else:
-                later = scores_of(jnp.minimum(g + 1, kv_heads - 1), 0)
+                later = scores_of(jnp.minimum((i + 1) * step, kv_heads - 1), 0)
             finish(g, part, scores)
             scores = later
         ahead_ref[...] = scores
         return 0
 
-    lax.fori_loop(0, kv_heads, one_head, 0)
+    lax.fori_loop(0, kv_heads // step, some_heads, 0)
 
 
 def pick_kernel(place_ref, q_ref, out_ref, sem):
@@ -237,14 +239,22 @@
     width = qt_ref.shape[1] // (2 * kv_heads * PARTS)
     out = out_ref
     if refs:
-        out, sem = refs
+        out, sems = refs
 
     def load(at):
         return max_ref[:1, at], acc_ref[:, at]
+
+    def copy_out(piece):
+        whole = place_ref[2] * (kv_heads * PARTS) + piece
+        return pltpu.make_async_copy(
+            out.at[:, lanes(piece, width)], out_ref.at[:, lanes(whole, width)], sems.at[piece]
+        )
 
     def finish(g, part, at, row_max, acc):
         finished = (acc[:HD] * (1.0 / acc[HD : HD + 1])).astype(out.dtype)
         out[:, lanes(g * PARTS + part, width)] = turned(finished, width // rows)
+        if refs:
+            copy_out(g * PARTS + part).start()
 
     needed = span_steps(place_ref, lengths_ref, kv_ref, qt_ref, ahead_ref, number, side, load, finish)
 
@@ -258,16 +268,25 @@
         lax.fori_loop(0, kv_heads, one_head, 0)
 
     if refs:
-        copy = pltpu.make_async_copy(out, out_ref.at[:, lanes(place_ref[2], out.shape[1])], sem)
+        for piece in range(kv_heads * PARTS):
+            copy_out(piece).wait()
+
+
+def join_kernel(place_ref, far_ref, out_in, out_ref, sems):
+    del out_in
+    pieces = sems.shape[0]
+    rows = far_ref.shape[0] // pieces
+    columns = lanes(1 - place_ref[2], far_ref.shape[1])
+    copies = [
+        pltpu.make_async_copy(
+            far_ref.at[pl.ds(i * rows, rows), :], out_ref.at[pl.ds(i * rows, rows), columns], sems.at[i]
+        )
+        for i in range(pieces)
+    ]
+    for copy in copies:
         copy.start()
+    for copy in copies:
         copy.wait()
-
-
-def join_kernel(place_ref, far_ref, out_in, out_ref, sem):
-    del out_in
-    copy = pltpu.make_async_copy(far_ref, out_ref.at[:, lanes(1 - place_ref[2], far_ref.shape[1])], sem)
-    copy.start()
-    copy.wait()
 
 
 def per_device(queries, keys, values, doc_lengths):
@@ -367,22 +386,21 @@
             **common,
         )(place, doc_lengths, *kv, qt, row_max, acc)
 
-    arrived[0], arrived[1], acc = lax.optimization_barrier((arrived[0], arrived[1], acc))
-    behind = jnp.where(half == 0, arrived[0], arrived[1])
-    opposite = jnp.where(half == 0, arrived[1], arrived[0])
-
-    def to_send(kind):
-        if kind == SHIFT_OPPOSITE:
-            return opposite
-        return jnp.where((place_in_group ^ kind) > place_in_group, own, behind)
-
-    for kinds in ROUNDS[2:]:
-        arrived.append(send_round(jnp.where(half == 0, to_send(kinds[0]), to_send(kinds[1])), kinds))
-    row_max, acc = attend(arrived[:2], row_max, acc, 0)
-    row_max, acc = attend(arrived[2:3], row_max, acc, 2)
-    row_max, acc = attend(arrived[3:4], row_max, acc, 3)
-
-    last_args = (place, doc_lengths, arrived[4], qt, row_max, acc)
+    behind, opposite, acc = lax.optimization_barrier((arrived[0], arrived[1], acc))
+
+    def plane_round(number):
+        sends = [jnp.where((place_in_group ^ kind) > place_in_group, own, behind) for kind in ROUNDS[number]]
+        return jnp.where(half == 0, *sends)
+
+    first = send_round(plane_round(2), ROUNDS[2])
+    relayed = send_round(opposite, ROUNDS[3])
+    row_max, acc = attend([behind, opposite], row_max, acc, 0)
+    to_second, acc = lax.optimization_barrier((plane_round(4), acc))
+    second = send_round(to_second, ROUNDS[4])
+    row_max, acc = attend([first], row_max, acc, 2)
+    row_max, acc = attend([relayed], row_max, acc, 3)
+
+    last_args = (place, doc_lengths, second, qt, row_max, acc)
     out_far = pl.pallas_call(
         functools.partial(last_kernel, number=4, side=1),
         in_specs=[smem, smem] + [vmem] * 4,
@@ -397,7 +415,11 @@
         in_specs=[smem, smem] + [vmem] * 4,
         out_specs=anywhere,
         out_shape=jax.ShapeDtypeStruct(queries.shape, queries.dtype),
-        scratch_shapes=[ahead, pltpu.VMEM((rows, half_heads), queries.dtype), pltpu.SemaphoreType.DMA],
+        scratch_shapes=[
+            ahead,
+            pltpu.VMEM((rows, half_heads), queries.dtype),
+            pltpu.SemaphoreType.DMA((half_heads // group_columns,)),
+        ],
         name="attend_last_near",
         **common,
     )(*last_args)
@@ -407,7 +429,7 @@
         out_specs=anywhere,
         out_shape=jax.ShapeDtypeStruct(queries.shape, queries.dtype),
         input_output_aliases={2: 0},
-        scratch_shapes=[pltpu.SemaphoreType.DMA],
+        scratch_shapes=[pltpu.SemaphoreType.DMA((rows // 16,))],
         name="join_heads",
         **common,
     )(place, to_other_core(out_far), out)

time: 53.4 us -> 51.1 us (0.957)
  the two profiles are of different devices: /device:TPU:7 before, /device:TPU:16 now
where the time goes in v1:
time: 51.1 us; the launch traced here: 51.9 us
  Pallas kernels  32.4 us (63%)
  starting transfers between devices  9.75 us (19%)
  waiting for transfers between devices  7.82 us (15%)
  local copies, waits for them, and re-layouts  1.37 us (3%)
    pallas_call x3, Pallas kernels, attend(): pl.pallas_call(functools.partial(span_kernel, numbers=tuple(range(number,...  16.7 us
    ppermute x5, starting transfers between devices, send_round(): return lax.ppermute(block, AXES, pairs)  9.53 us
    ppermute x5, waiting for transfers between devices, send_round(): return lax.ppermute(block, AXES, pairs)  6.47 us
    pallas_call x1, Pallas kernels, per_device(): pl.pallas_call(functools.partial(last_kernel, number=4, side=0), in_specs...  3.89 us
    pallas_call x1, Pallas kernels, per_device(): pl.pallas_call(functools.partial(last_kernel, number=4, side=1), in_specs...  3.46 us
    pallas_call x1, Pallas kernels, per_device(): pl.pallas_call(functools.partial(own_kernel, side=1), in_specs=[smem, sme...  3.23 us
    pallas_call x1, Pallas kernels, per_device(): pl.pallas_call(functools.partial(own_kernel, side=0), in_specs=[smem, sme...  2.82 us
    pallas_call x1, Pallas kernels, per_device(): pl.pallas_call(join_kernel, in_specs=[smem, vmem, anywhere], out_specs=an...  1.57 us
  transfers between devices with their start and end apart: 8, of which 4 were waited for; matrix products, arithmetic and copies ran while one was open for 0% of the time, Pallas kernels for 53%

profile of v1, /device:TPU:16, one launch (start us, length us, event | category | flops | bytes accessed | tf_op | source)
XLA Modules:
  0.0 51.9 jit_solution(17597680737854102399)
XLA Ops:
  0.0 0.0 copy-start
  0.0 0.0 copy-start.1
  0.0 1.3 %dynamic-slice_bitcast_fusion.2 = (bf16[1,128,512]{2,1,0:T(8,128)(2,1)S(1)}, bf16[1,128,512]{2,1,0:T(8,128)(2,1)S(1)}, bf16[1,128,512]{2,1,0:T(8,128)(2,1)S(1)}, bf16[1,128,512]{2,1,0:T(8,128)(2,1)S(1)}) fusion(bf16[128,1024]{1,0:T(8,128)(2,1)} %param.6, s32[]{:T(128)S(6)} %select_n.73, s32[]{:T(128)S(6)} %select_n.74, bf16[128,1024]{1,0:T(8,128)(2,1)} %param.5), kind=kLoop, calls=%fused_computation.9 | loop fusion | bytes 1048584 | tf_op jit(solution)/shard_map/stack | solution.py:340
  1.3 0.1 collective-permute-start
  1.5 0.1 stack.82.place_ref
  1.6 1.3 %collective-permute-done = bf16[2,128,512]{2,1,0:T(8,128)(2,1)S(1)} collective-permute-done((bf16[2,128,512]{2,1,0:T(8,128)(2,1)S(1)}, bf16[2,128,512]{2,1,0:T(8,128)(2,1)S(1)}, u32[]{:S(2)}, u32[]{:S(2)}) %collective-permute-start) | collective-permute-done | bytes 262176 | tf_op jit(solution)/shard_map/ppermute | solution.py:39
  2.9 0.1 pad_maximum_fusion.kv_ref
  3.0 3.5 %collective-permute-start.1 = (bf16[2,2,128,512]{3,2,1,0:T(8,128)(2,1)S(1)}, bf16[2,2,128,512]{3,2,1,0:T(8,128)(2,1)S(1)}, u32[]{:S(2)}, u32[]{:S(2)}) collective-permute-start(bf16[2,2,128,512]{3,2,1,0:T(8,128)(2,1)S(1)} %pad_maximum_fusion.kv_ref), channel_id=1, source_target_pairs={{0,8},{1,9},{2,10},{3,11},{4,12},{5,13},{6,14},{7,15},{8,16},{9,17... | collective-permute-start | bytes 1572872 | tf_op jit(solution)/shard_map/ppermute | solution.py:34
  6.5 2.5 %collective-permute-start.2 = (bf16[2,2,128,512]{3,2,1,0:T(8,128)(2,1)S(1)}, bf16[2,2,128,512]{3,2,1,0:T(8,128)(2,1)S(1)}, u32[]{:S(2)}, u32[]{:S(2)}) collective-permute-start(bf16[2,2,128,512]{3,2,1,0:T(8,128)(2,1)S(1)} %pad_maximum_fusion.kv_ref), channel_id=1, source_target_pairs={{0,6},{1,7},{2,4},{3,5},{4,2},{5,3},{6,0},{7,1},{8,14},{9,15},{10,... | collective-permute-start | bytes 1572872 | tf_op jit(solution)/shard_map/ppermute | solution.py:34
  9.0 0.0 copy-done
  9.0 0.6 %pick_queries.1 = bf16[128,4096]{1,0:T(8,128)(2,1)S(1)} custom-call(s32[13]{0:T(128)S(1)} %stack.82.place_ref, bf16[128,8192]{1,0:T(8,128)(2,1)S(1)} %copy-done), custom_call_target="tpu_custom_call" | custom-call | tf_op jit(solution)/shard_map/pick_queries/pallas_call | solution.py:343
  9.6 0.1 collective-permute-start.3
  9.7 0.0 copy-done.1
  9.7 2.8 %attend_own_near.1 = (bf16[128,8192]{1,0:T(8,128)(2,1)S(1)}, f32[8,8192]{1,0:T(8,128)S(1)}, f32[144,8192]{1,0:T(8,128)S(1)}) custom-call(s32[13]{0:T(128)S(1)} %stack.82.place_ref, s32[12]{0:T(128)S(1)} %copy-done.1, bf16[128,8192]{1,0:T(8,128)(2,1)S(1)} %copy-done, bf16[2,2,128,512]{3,2,1,0:T(8,128)(2,1)S(1)} %pad_maximum_fusion.kv_ref), custom_call_target="tpu_custom_call" | custom-call | flops 99999997952 | tf_op jit(solution)/shard_map/attend_own_near/pallas_call | solution.py:357
  12.5 0.0 collective-permute-done.3.q_ref
  12.5 3.2 %attend_own_far.1 = (bf16[128,8192]{1,0:T(8,128)(2,1)S(1)}, f32[8,8192]{1,0:T(8,128)S(1)}, f32[144,8192]{1,0:T(8,128)S(1)}) custom-call(s32[13]{0:T(128)S(1)} %stack.82.place_ref, s32[12]{0:T(128)S(1)} %copy-done.1, bf16[128,4096]{1,0:T(8,128)(2,1)S(1)} %collective-permute-done.3.q_ref, ...), custom_call_target="tpu_custom_call", output_to_operand_aliasing={{0}: (4, {}), {1}: (5, {}), {2}: (6, {})} | custom-call | tf_op jit(solution)/shard_map/attend_own_far/pallas_call | solution.py:366
  15.8 3.1 %collective-permute-done.1.refs_0_ = bf16[2,2,128,512]{3,2,1,0:T(8,128)(2,1)S(1)} collective-permute-done((bf16[2,2,128,512]{3,2,1,0:T(8,128)(2,1)S(1)}, bf16[2,2,128,512]{3,2,1,0:T(8,128)(2,1)S(1)}, u32[]{:S(2)}, u32[]{:S(2)}) %collective-permute-start.1) | collective-permute-done | bytes 524320 | tf_op jit(solution)/shard_map/ppermute | solution.py:34
  18.8 2.3 %collective-permute-done.2.refs_1_ = bf16[2,2,128,512]{3,2,1,0:T(8,128)(2,1)S(1)} collective-permute-done((bf16[2,2,128,512]{3,2,1,0:T(8,128)(2,1)S(1)}, bf16[2,2,128,512]{3,2,1,0:T(8,128)(2,1)S(1)}, u32[]{:S(2)}, u32[]{:S(2)}) %collective-permute-start.2) | collective-permute-done | bytes 524320 | tf_op jit(solution)/shard_map/ppermute | solution.py:34
  21.1 0.1 broadcast_select_fusion.2
  21.2 1.6 %collective-permute-start.6 = (bf16[2,2,128,512]{3,2,1,0:T(8,128)(2,1)S(1)}, bf16[2,2,128,512]{3,2,1,0:T(8,128)(2,1)S(1)}, u32[]{:S(2)}, u32[]{:S(2)}) collective-permute-start(bf16[2,2,128,512]{3,2,1,0:T(8,128)(2,1)S(1)} %get-tuple-element.43), channel_id=1, source_target_pairs={{0,2},{1,5},{2,0},{3,7},{4,6},{5,1},{6,4},{7,3},{8,10},{9,13},{10,... | collective-permute-start | bytes 1572872 | tf_op jit(solution)/shard_map/ppermute | solution.py:34
  22.8 1.9 %collective-permute-start.5 = (bf16[2,2,128,512]{3,2,1,0:T(8,128)(2,1)S(1)}, bf16[2,2,128,512]{3,2,1,0:T(8,128)(2,1)S(1)}, u32[]{:S(2)}, u32[]{:S(2)}) collective-permute-start(bf16[2,2,128,512]{3,2,1,0:T(8,128)(2,1)S(1)} %collective-permute-done.2.refs_1_), channel_id=1, source_target_pairs={{0,8},{1,9},{2,10},{3,11},{8,16},{9,17},{10,18},{11,19},{16,24},{1... | collective-permute-start | bytes 1572872 | tf_op jit(solution)/shard_map/ppermute | solution.py:34
  24.7 5.8 %attend_spans.3 = (f32[8,8192]{1,0:T(8,128)S(1)}, f32[144,8192]{1,0:T(8,128)S(1)}) custom-call(s32[13]{0:T(128)S(1)} %stack.82.place_ref, s32[12]{0:T(128)S(1)} %copy-done.1, bf16[2,2,128,512]{3,2,1,0:T(8,128)(2,1)S(1)} %collective-permute-done.1.refs_0_, ...), custom_call_target="tpu_custom_call", output_to_operand_aliasing={{0}: (5, {}), {1}: (6, {})} | custom-call | tf_op jit(solution)/shard_map/attend_spans/pallas_call | solution.py:378
  30.5 0.1 collective-permute-start.4
  30.6 0.0 collective-permute-done.6.refs_0_
  30.6 5.5 %attend_spans.4 = (f32[8,8192]{1,0:T(8,128)S(1)}, f32[144,8192]{1,0:T(8,128)S(1)}) custom-call(s32[13]{0:T(128)S(1)} %stack.82.place_ref, s32[12]{0:T(128)S(1)} %copy-done.1, bf16[2,2,128,512]{3,2,1,0:T(8,128)(2,1)S(1)} %collective-permute-done.6.refs_0_, ...), custom_call_target="tpu_custom_call", output_to_operand_aliasing={{0}: (4, {}), {1}: (5, {})} | custom-call | tf_op jit(solution)/shard_map/attend_spans/pallas_call | solution.py:378
  36.1 1.1 %collective-permute-done.5.refs_0_ = bf16[2,2,128,512]{3,2,1,0:T(8,128)(2,1)S(1)} collective-permute-done((bf16[2,2,128,512]{3,2,1,0:T(8,128)(2,1)S(1)}, bf16[2,2,128,512]{3,2,1,0:T(8,128)(2,1)S(1)}, u32[]{:S(2)}, u32[]{:S(2)}) %collective-permute-start.5) | collective-permute-done | bytes 524320 | tf_op jit(solution)/shard_map/ppermute | solution.py:34
  37.2 5.5 %attend_spans.5 = (f32[8,8192]{1,0:T(8,128)S(1)}, f32[144,8192]{1,0:T(8,128)S(1)}) custom-call(s32[13]{0:T(128)S(1)} %stack.82.place_ref, s32[12]{0:T(128)S(1)} %copy-done.1, bf16[2,2,128,512]{3,2,1,0:T(8,128)(2,1)S(1)} %collective-permute-done.5.refs_0_, ...), custom_call_target="tpu_custom_call", output_to_operand_aliasing={{0}: (4, {}), {1}: (5, {})} | custom-call | tf_op jit(solution)/shard_map/attend_spans/pallas_call | solution.py:378
  42.7 0.0 collective-permute-done.4.kv_ref
  42.7 3.5 %attend_last_far.1 = bf16[128,4096]{1,0:T(8,128)(2,1)S(1)} custom-call(s32[13]{0:T(128)S(1)} %stack.82.place_ref, s32[12]{0:T(128)S(1)} %copy-done.1, bf16[2,2,128,512]{3,2,1,0:T(8,128)(2,1)S(1)} %collective-permute-done.4.kv_ref, bf16[128,8192]{1,0:T(8,128)(2,1)S(1)} %get-tuple-element.32.refs_2_.refs_1_.qt_ref, f32[8,8192]{1,0:T(8,128)S(1)} %get-tuple-element.41.max_ref, ...), custom_call_target="tpu_custom_call" | custom-call | tf_op jit(solution)/shard_map/attend_last_far/pallas_call | solution.py:404
  46.2 0.1 collective-permute-start.7
  46.2 3.9 %attend_last_near.1.out_in = bf16[128,8192]{1,0:T(8,128)(2,1)} custom-call(s32[13]{0:T(128)S(1)} %stack.82.place_ref, s32[12]{0:T(128)S(1)} %copy-done.1, bf16[2,2,128,512]{3,2,1,0:T(8,128)(2,1)S(1)} %collective-permute-done.4.kv_ref, bf16[128,8192]{1,0:T(8,128)(2,1)S(1)} %get-tuple-element.32.refs_2_.refs_1_.qt_ref, ...), custom_call_target="tpu_custom_call" | custom-call | tf_op jit(solution)/shard_map/attend_last_near/pallas_call | solution.py:413
  50.1 0.0 collective-permute-done.7.far_ref
  50.1 1.6 %join_heads.1 = bf16[128,8192]{1,0:T(8,128)(2,1)} custom-call(s32[13]{0:T(128)S(1)} %stack.82.place_ref, bf16[128,4096]{1,0:T(8,128)(2,1)S(1)} %collective-permute-done.7.far_ref, bf16[128,8192]{1,0:T(8,128)(2,1)} %attend_last_near.1.out_in), custom_call_target="tpu_custom_call", output_to_operand_aliasing={{}: (2, {})} | custom-call | tf_op jit(solution)/shard_map/join_heads/pallas_call | solution.py:426
  (2 shorter events, 0.1 us)
Async XLA Ops:
  0.0 9.0 %copy-start = (bf16[128,8192]{1,0:T(8,128)(2,1)S(1)}, bf16[128,8192]{1,0:T(8,128)(2,1)}, u32[]{:S(2)}) copy-start(bf16[128,8192]{1,0:T(8,128)(2,1)} %q_ref.1) | copy-start | bytes 6291460
  0.0 9.7 %copy-start.1 = (s32[12]{0:T(128)S(1)}, s32[12]{0:T(128)}, u32[]{:S(2)}) copy-start(s32[12]{0:T(128)} %lengths_ref.13) | copy-start | bytes 148
  1.3 1.6 %collective-permute-start = (bf16[2,128,512]{2,1,0:T(8,128)(2,1)S(1)}, bf16[2,128,512]{2,1,0:T(8,128)(2,1)S(1)}, u32[]{:S(2)}, u32[]{:S(2)}) collective-permute-start(bf16[2,128,512]{2,1,0:T(8,128)(2,1)S(1)} %pad_maximum_fusion.1), channel_id=1, source_target_pairs={{0,1},{1,0},{2,3},{3,2},{4,5},{5,4},{6,7},{7,6},{8,9},{9,8},{10,11... | collective-permute-start | bytes 786440 | tf_op jit(solution)/shard_map/ppermute | solution.py:39
  3.0 15.9 %collective-permute-start.1 = (bf16[2,2,128,512]{3,2,1,0:T(8,128)(2,1)S(1)}, bf16[2,2,128,512]{3,2,1,0:T(8,128)(2,1)S(1)}, u32[]{:S(2)}, u32[]{:S(2)}) collective-permute-start(bf16[2,2,128,512]{3,2,1,0:T(8,128)(2,1)S(1)} %pad_maximum_fusion.kv_ref), channel_id=1, source_target_pairs={{0,8},{1,9},{2,10},{3,11},{4,12},{5,13},{6,14},{7,15},{8,16},{9,17... | collective-permute-start | bytes 1572872 | tf_op jit(solution)/shard_map/ppermute | solution.py:34
  6.5 14.6 %collective-permute-start.2 = (bf16[2,2,128,512]{3,2,1,0:T(8,128)(2,1)S(1)}, bf16[2,2,128,512]{3,2,1,0:T(8,128)(2,1)S(1)}, u32[]{:S(2)}, u32[]{:S(2)}) collective-permute-start(bf16[2,2,128,512]{3,2,1,0:T(8,128)(2,1)S(1)} %pad_maximum_fusion.kv_ref), channel_id=1, source_target_pairs={{0,6},{1,7},{2,4},{3,5},{4,2},{5,3},{6,0},{7,1},{8,14},{9,15},{10,... | collective-permute-start | bytes 1572872 | tf_op jit(solution)/shard_map/ppermute | solution.py:34
  9.6 2.9 %collective-permute-start.3 = (bf16[128,4096]{1,0:T(8,128)(2,1)S(1)}, bf16[128,4096]{1,0:T(8,128)(2,1)S(1)}, u32[]{:S(2)}, u32[]{:S(2)}) collective-permute-start(bf16[128,4096]{1,0:T(8,128)(2,1)S(1)} %pick_queries.1), channel_id=1, source_target_pairs={{0,1},{1,0},{2,3},{3,2},{4,5},{5,4},{6,7},{7,6},{8,9},{9,8},{10,11... | collective-permute-start | bytes 3145736 | tf_op jit(solution)/shard_map/ppermute | solution.py:39
  21.2 9.4 %collective-permute-start.6 = (bf16[2,2,128,512]{3,2,1,0:T(8,128)(2,1)S(1)}, bf16[2,2,128,512]{3,2,1,0:T(8,128)(2,1)S(1)}, u32[]{:S(2)}, u32[]{:S(2)}) collective-permute-start(bf16[2,2,128,512]{3,2,1,0:T(8,128)(2,1)S(1)} %get-tuple-element.43), channel_id=1, source_target_pairs={{0,2},{1,5},{2,0},{3,7},{4,6},{5,1},{6,4},{7,3},{8,10},{9,13},{10,... | collective-permute-start | bytes 1572872 | tf_op jit(solution)/shard_map/ppermute | solution.py:34
  22.8 14.4 %collective-permute-start.5 = (bf16[2,2,128,512]{3,2,1,0:T(8,128)(2,1)S(1)}, bf16[2,2,128,512]{3,2,1,0:T(8,128)(2,1)S(1)}, u32[]{:S(2)}, u32[]{:S(2)}) collective-permute-start(bf16[2,2,128,512]{3,2,1,0:T(8,128)(2,1)S(1)} %collective-permute-done.2.refs_1_), channel_id=1, source_target_pairs={{0,8},{1,9},{2,10},{3,11},{8,16},{9,17},{10,18},{11,19},{16,24},{1... | collective-permute-start | bytes 1572872 | tf_op jit(solution)/shard_map/ppermute | solution.py:34
  30.5 12.2 %collective-permute-start.4 = (bf16[2,2,128,512]{3,2,1,0:T(8,128)(2,1)S(1)}, bf16[2,2,128,512]{3,2,1,0:T(8,128)(2,1)S(1)}, u32[]{:S(2)}, u32[]{:S(2)}) collective-permute-start(bf16[2,2,128,512]{3,2,1,0:T(8,128)(2,1)S(1)} %get-tuple-element.36), channel_id=1, source_target_pairs={{0,4},{1,3},{2,6},{3,1},{4,0},{5,7},{6,2},{7,5},{8,12},{9,11},{10,... | collective-permute-start | bytes 1572872 | tf_op jit(solution)/shard_map/ppermute | solution.py:34
  46.2 4.0 %collective-permute-start.7 = (bf16[128,4096]{1,0:T(8,128)(2,1)S(1)}, bf16[128,4096]{1,0:T(8,128)(2,1)S(1)}, u32[]{:S(2)}, u32[]{:S(2)}) collective-permute-start(bf16[128,4096]{1,0:T(8,128)(2,1)S(1)} %attend_last_far.1), channel_id=1, source_target_pairs={{0,1},{1,0},{2,3},{3,2},{4,5},{5,4},{6,7},{7,6},{8,9},{9,8},{10,11... | collective-permute-start | bytes 3145736 | tf_op jit(solution)/shard_map/ppermute | solution.py:39
